TPU v7x, 512 devices: a whole 4x4x16 slice. The times are simulated.
512 devices in a mesh: frame: 128 (over y, z_lo, x), space: 4 (over z_hi, core).
Axes of the slice: x: 4, y: 4, z: 16 (z_hi: 2, z_lo: 8; z = z_hi * 8 + z_lo), core: 2. Of those that a mesh axis runs over, the one named last changes fastest.
Arguments:
- query_vectors: bfloat16 [512, 12, 12, 1024], P('frame', 'space'), may hold values from -6 to 6
- key_vectors: bfloat16 [512, 12, 12, 1024], P('frame', 'space'), may hold values from -6 to 6
- value_vectors: bfloat16 [512, 12, 12, 1024], P('frame', 'space'), may hold values from -6 to 6
- out_cotangent: bfloat16 [512, 12, 12, 1024], P('frame', 'space'), may hold values from -6 to 6
- partner_mask: int32 [512, 4], replicated, may hold values 0 or 1
Outputs:
- attended: bfloat16 [512, 12, 12, 1024], P('frame', 'space')
- query_grad: bfloat16 [512, 12, 12, 1024], P('frame', 'space')
- key_grad: bfloat16 [512, 12, 12, 1024], P('frame', 'space')
- value_grad: bfloat16 [512, 12, 12, 1024], P('frame', 'space')
All inputs are finite; a program needn't handle non-finite values.
Results may differ from a plain program's by a relative error of at most 0.011.
Values may be sent and summed in bfloat16 or wider, within the bound.
A program may use at most 128 MiB of HBM per device.

v0:
```python
import functools

import jax
import jax.numpy as jnp
from jax import lax
from jax.experimental import pallas as pl
from jax.experimental.pallas import tpu as pltpu
from jax.sharding import PartitionSpec as P

HEAD_DIM = 64
SCALE = 0.125
NEG = -1e30
WIDE = 256
HEADS = WIDE // HEAD_DIM
STATS = 3 * HEADS
F32 = jnp.float32
BF16 = jnp.bfloat16


def dot_nt(a, b):
    return lax.dot_general(a, b, (((1,), (1,)), ((), ())), preferred_element_type=F32)


def dot_nn(a, b):
    return lax.dot_general(a, b, (((1,), (0,)), ((), ())), preferred_element_type=F32)


def dot_tn(a, b):
    return lax.dot_general(a, b, (((0,), (0,)), ((), ())), preferred_element_type=F32)


def kernel(
    dims, kv_ref, qg_ref, bias_ref, o_ref, dq_ref, dk_ref, dv_ref,
    kvx, halo, qm, gm, pm, ot, stat, stat_in, wm, dm, oq, rim_out, rim_in, dkv, dkv_out, dkv_in,
    kv_ss, kv_rs, halo_ss, halo_rs, stat_ss, stat_rs, rim_ss, rim_rs, dkv_ss, dkv_rs,
):
    chunks, rows, tok, bits, space, keys = dims
    ext = rows + 2
    frame_at = lax.axis_index("frame")
    space_at = lax.axis_index("space")
    partner = []
    for b in range(bits):
        step = 1 << b
        partner.append(frame_at + step * (1 - 2 * ((frame_at // step) % 2)))
    has = (space_at > 0, space_at < space - 1)
    near = (space_at - 1, space_at + 1)

    def remote(src, dst, send, recv, frame, band):
        return pltpu.make_async_remote_copy(
            src_ref=src, dst_ref=dst, send_sem=send, recv_sem=recv,
            device_id=(frame, band), device_id_type=pl.DeviceIdType.MESH,
        )

    def kv_copy(c, b):
        return remote(
            kv_ref.at[c], kvx.at[c, :, :, pl.ds(tok * (b + 1), tok)],
            kv_ss.at[c, b], kv_rs.at[c, b], partner[b], space_at,
        )

    def dkv_copy(c, b):
        return remote(
            dkv_out.at[c, b], dkv_in.at[c, b], dkv_ss.at[c, b], dkv_rs.at[c, b], partner[b], space_at
        )

    def halo_copy(c, s):
        return remote(
            qg_ref.at[c, :, 0 if s == 0 else rows - 1], halo.at[c, 1 - s],
            halo_ss.at[c, s], halo_rs.at[c, 1 - s], frame_at, near[s],
        )

    def stat_copy(c, s):
        return remote(
            stat.at[c, 2 * s], stat_in.at[c, 1 - s],
            stat_ss.at[c, s], stat_rs.at[c, 1 - s], frame_at, near[s],
        )

    def rim_copy(c, s):
        return remote(
            rim_out.at[c, s], rim_in.at[c, 1 - s],
            rim_ss.at[c, s], rim_rs.at[c, 1 - s], frame_at, near[s],
        )

    def start_sides(copy, c):
        for s in range(2):
            @pl.when(has[s])
            def _():
                copy(c, s).start()

    def wait_sides(copy, c):
        for s in range(2):
            @pl.when(has[s])
            def _():
                copy(c, 1 - s).wait_recv()

    def wait_sent_sides(copy, c):
        for s in range(2):
            @pl.when(has[s])
            def _():
                copy(c, s).wait_send()

    barrier = pltpu.get_barrier_semaphore()
    for b in range(bits):
        pl.semaphore_signal(
            barrier, inc=1, device_id=(partner[b], space_at), device_id_type=pl.DeviceIdType.MESH
        )
    for s in range(2):
        @pl.when(has[s])
        def _():
            pl.semaphore_signal(
                barrier, inc=1, device_id=(frame_at, near[s]), device_id_type=pl.DeviceIdType.MESH
            )
    pl.semaphore_wait(barrier, bits + has[0].astype(jnp.int32) + has[1].astype(jnp.int32))

    def send_first(c, carry):
        for b in reversed(range(bits)):
            kv_copy(c, b).start()
        start_sides(halo_copy, c)
        return carry

    lax.fori_loop(0, chunks, send_first, 0)

    lane = lax.broadcasted_iota(jnp.int32, (tok, 128), 1)
    low = lane < HEAD_DIM

    for s in range(2):
        @pl.when(jnp.logical_not(has[s]))
        def _():
            halo[:, s] = jnp.zeros(halo.shape[:1] + halo.shape[2:], BF16)
            rim_in[:, s] = jnp.zeros(rim_in.shape[:1] + rim_in.shape[2:], BF16)
            top_lane = lane - (lane // STATS) * STATS < HEADS
            stat_in[:, s] = jnp.broadcast_to(
                jnp.where(top_lane, NEG, 0.0).astype(F32)[None], (chunks, tok, 128)
            )

    def stacked(block):
        wide = block.astype(F32)
        zero = jnp.zeros((tok, 128), F32)
        out = []
        for h in range(HEADS):
            half = wide[:, 128 * (h // 2) : 128 * (h // 2) + 128]
            kept = jnp.where(low if h % 2 == 0 else jnp.logical_not(low), half, zero)
            out.append(jnp.concatenate([kept, zero] if h < 2 else [zero, kept], axis=1))
        return jnp.concatenate(out, axis=0).astype(BF16)

    def picked(full):
        return jnp.concatenate(
            [
                jnp.where(low, full[:tok, :128], full[tok : 2 * tok, :128]),
                jnp.where(low, full[2 * tok : 3 * tok, 128:], full[3 * tok :, 128:]),
            ],
            axis=1,
        )

    def forward(c):
        kvx[c, :, :, :tok, :] = kv_ref[c]
        spare = keys - tok * (bits + 1)
        if spare:
            kvx[c, :, :, keys - spare :, :] = jnp.zeros((2, rows, spare, WIDE), BF16)
        bias = jnp.concatenate([bias_ref[...]] * HEADS, axis=0)
        tiles = [jnp.zeros((tok, 128), F32) for _ in range(3)]
        for i in range(ext):
            if i == 0 or i == ext - 1:
                query, grad = halo[c, 0 if i == 0 else 1, 0], halo[c, 0 if i == 0 else 1, 1]
            else:
                query, grad = qg_ref[c, 0, i - 1], qg_ref[c, 1, i - 1]
            query = stacked(query)
            grad = stacked(grad)
            qm[c, i] = query
            gm[c, i] = grad
            near_rows = [r for r in range(rows) if 0 <= i - r <= 2]
            scores = [dot_nt(query, kvx[c, 0, r]) + bias for r in near_rows]
            top = jnp.max(functools.reduce(jnp.maximum, scores), axis=1, keepdims=True)
            probs = [jnp.exp(one - top) for one in scores]
            total = jnp.sum(functools.reduce(jnp.add, probs), axis=1, keepdims=True)
            full = None
            for r, prob in zip(near_rows, probs):
                prob = prob.astype(BF16)
                pm[c, r, i - r] = prob
                part = dot_nn(prob, kvx[c, 1, r])
                full = part if full is None else full + part
            ot[c, i] = picked(full)
            place = 0 if i < 2 else (1 if i < ext - 2 else 2)
            base = STATS * (1 if i in (1, ext - 1) else 0)
            for h in range(HEADS):
                span = slice(h * tok, (h + 1) * tok)
                half = slice(128 * (h // 2), 128 * (h // 2) + 128)
                delta = jnp.sum(
                    full[span, half] * grad[span, half].astype(F32), axis=1, keepdims=True
                )
                for kind, value in enumerate((top[span], total[span], delta)):
                    tiles[place] = jnp.where(lane == base + kind * HEADS + h, value, tiles[place])
        for place in range(3):
            stat[c, place] = tiles[place]

    def backward(c):
        alphas, deltas = [], []
        for place in range(3):
            mine = stat[c, place]
            top, total, delta = mine, pltpu.roll(mine, 128 - HEADS, 1), pltpu.roll(mine, 128 - 2 * HEADS, 1)
            if place == 1:
                alphas.append(1.0 / total)
                deltas.append(delta / total)
                continue
            theirs = stat_in[c, 0 if place == 0 else 1]
            top2, total2, delta2 = (
                theirs, pltpu.roll(theirs, 128 - HEADS, 1), pltpu.roll(theirs, 128 - 2 * HEADS, 1)
            )
            best = jnp.maximum(top, top2)
            part, part2 = jnp.exp(top - best), jnp.exp(top2 - best)
            inverse = 1.0 / (total * part + total2 * part2)
            alphas.append(part * inverse)
            deltas.append((delta * part + delta2 * part2) * inverse)
        for i in range(ext):
            place = 0 if i < 2 else (1 if i < ext - 2 else 2)
            base = STATS * (1 if i in (1, ext - 1) else 0)
            alpha_h = [alphas[place][:, base + h : base + h + 1] for h in range(HEADS)]
            alpha = jnp.concatenate(alpha_h, axis=0)
            delta = jnp.concatenate(
                [deltas[place][:, base + h : base + h + 1] for h in range(HEADS)], axis=0
            )
            full = None
            for r in range(rows):
                if not 0 <= i - r <= 2:
                    continue
                grad_prob = dot_nt(gm[c, i], kvx[c, 1, r])
                weight = pm[c, r, i - r].astype(F32) * alpha
                grad_score = (weight * (grad_prob - delta)).astype(BF16)
                wm[r, i - r] = weight.astype(BF16)
                dm[r, i - r] = grad_score
                part = dot_nn(grad_score, kvx[c, 0, r])
                full = part if full is None else full + part
            query_grad = picked(full) * SCALE
            spread = jnp.concatenate(
                [jnp.where(low, alpha_h[0], alpha_h[1]), jnp.where(low, alpha_h[2], alpha_h[3])], axis=1
            )
            attended = ot[c, i] * spread
            if i == 0 or i == ext - 1:
                s = 0 if i == 0 else 1
                rim_out[c, s, 0] = attended.astype(BF16)
                rim_out[c, s, 1] = query_grad.astype(BF16)
            else:
                oq[c, 0, i - 1] = attended
                oq[c, 1, i - 1] = query_grad
        for r in range(rows):
            grads = gm[c, r : r + 3].reshape(3 * HEADS * tok, WIDE)
            queries = qm[c, r : r + 3].reshape(3 * HEADS * tok, WIDE)
            key_grad = dot_tn(dm[r].reshape(3 * HEADS * tok, keys), queries)
            value_grad = dot_tn(wm[r].reshape(3 * HEADS * tok, keys), grads)
            for which, result in enumerate((key_grad, value_grad)):
                dkv[c, which, r] = result[:tok]
                for b in range(bits):
                    dkv_out[c, b, which, r] = result[tok * (b + 1) : tok * (b + 2)].astype(BF16)

    def step(t, carry):
        @pl.when(t < chunks)
        def _():
            for b in range(bits):
                kv_copy(t, b).wait_recv()
            wait_sides(halo_copy, t)
            forward(t)
            start_sides(stat_copy, t)

        @pl.when(t > 0)
        def _():
            wait_sides(stat_copy, t - 1)
            backward(t - 1)
            for b in reversed(range(bits)):
                dkv_copy(t - 1, b).start()
            start_sides(rim_copy, t - 1)

        return carry

    lax.fori_loop(0, chunks + 1, step, 0)

    def finish(c, carry):
        wait_sides(rim_copy, c)
        for r in range(rows):
            for which, out in enumerate((o_ref, dq_ref)):
                result = oq[c, which, r]
                if r == 0:
                    result = result + rim_in[c, 0, which].astype(F32)
                if r == rows - 1:
                    result = result + rim_in[c, 1, which].astype(F32)
                out[c, r] = result.astype(BF16)
        for b in range(bits):
            dkv_copy(c, b).wait_recv()
        for r in range(rows):
            for which, out in enumerate((dk_ref, dv_ref)):
                result = dkv[c, which, r]
                for b in range(bits):
                    result = result + dkv_in[c, b, which, r].astype(F32)
                out[c, r] = result.astype(BF16)
        return carry

    lax.fori_loop(0, chunks, finish, 0)

    def drain(c, carry):
        for b in range(bits):
            kv_copy(c, b).wait_send()
            dkv_copy(c, b).wait_send()
        wait_sent_sides(halo_copy, c)
        wait_sent_sides(stat_copy, c)
        wait_sent_sides(rim_copy, c)
        return carry

    lax.fori_loop(0, chunks, drain, 0)


def per_device(query_vectors, key_vectors, value_vectors, out_cotangent, partner_mask):
    frames, rows, cols, width = query_vectors.shape
    bits = min(4, lax.axis_size("frame").bit_length() - 1)
    space = lax.axis_size("space")
    chunks = width // WIDE
    tok = frames * cols
    keys = -(-tok * (bits + 1) // 128) * 128
    ext = rows + 2

    def lay(array):
        return array.reshape(frames, rows, cols, chunks, WIDE).transpose(3, 1, 0, 2, 4).reshape(
            chunks, rows, tok, WIDE
        )

    def back(array):
        return array.reshape(chunks, rows, frames, cols, WIDE).transpose(2, 1, 3, 0, 4).reshape(
            frames, rows, cols, width
        )

    kv = jnp.stack([lay(key_vectors), lay(value_vectors)], axis=1)
    qg = jnp.stack([lay(query_vectors * SCALE), lay(out_cotangent)], axis=1)
    own = lax.dynamic_slice_in_dim(partner_mask, lax.axis_index("frame") * frames, frames, 0)[:, :bits] == 1
    allowed = jnp.concatenate([jnp.ones((frames, 1), bool), own], axis=1)
    allowed = jnp.repeat(jnp.repeat(allowed, cols, axis=0), tok, axis=1)
    allowed = jnp.pad(allowed, ((0, 0), (0, keys - allowed.shape[1])))
    bias = jnp.where(allowed, 0.0, NEG).astype(F32)

    dims = (chunks, rows, tok, bits, space, keys)
    out = jax.ShapeDtypeStruct((chunks, rows, tok, WIDE), BF16)
    vmem = pl.BlockSpec(memory_space=pltpu.VMEM)
    stack = HEADS * tok
    dma = pltpu.SemaphoreType.DMA
    results = pl.pallas_call(
        functools.partial(kernel, dims),
        out_shape=(out,) * 4,
        in_specs=[vmem] * 3,
        out_specs=(vmem,) * 4,
        scratch_shapes=[
            pltpu.VMEM((chunks, 2, rows, keys, WIDE), BF16),
            pltpu.VMEM((chunks, 2, 2, tok, WIDE), BF16),
            pltpu.VMEM((chunks, ext, stack, WIDE), BF16),
            pltpu.VMEM((chunks, ext, stack, WIDE), BF16),
            pltpu.VMEM((chunks, rows, 3, stack, keys), BF16),
            pltpu.VMEM((chunks, ext, tok, WIDE), F32),
            pltpu.VMEM((chunks, 3, tok, 128), F32),
            pltpu.VMEM((chunks, 2, tok, 128), F32),
            pltpu.VMEM((rows, 3, stack, keys), BF16),
            pltpu.VMEM((rows, 3, stack, keys), BF16),
            pltpu.VMEM((chunks, 2, rows, tok, WIDE), F32),
            pltpu.VMEM((chunks, 2, 2, tok, WIDE), BF16),
            pltpu.VMEM((chunks, 2, 2, tok, WIDE), BF16),
            pltpu.VMEM((chunks, 2, rows, tok, WIDE), F32),
            pltpu.VMEM((chunks, bits, 2, rows, tok, WIDE), BF16),
            pltpu.VMEM((chunks, bits, 2, rows, tok, WIDE), BF16),
            dma((chunks, bits)), dma((chunks, bits)),
            dma((chunks, 2)), dma((chunks, 2)),
            dma((chunks, 2)), dma((chunks, 2)),
            dma((chunks, 2)), dma((chunks, 2)),
            dma((chunks, bits)), dma((chunks, bits)),
        ],
        compiler_params=pltpu.CompilerParams(
            collective_id=0, has_side_effects=True, vmem_limit_bytes=56 * 1024 * 1024
        ),
        name="butterfly",
    )(kv, qg, bias)
    return tuple(back(result) for result in results)


def solution(mesh):
    spread = P("frame", "space", None, None)
    return jax.shard_map(
        per_device,
        mesh=mesh,
        in_specs=(spread,) * 4 + (P(),),
        out_specs=(spread,) * 4,
        check_vma=False,
    )
```

profile of v0, /device:TPU:67, one launch (start us, length us, event | category | flops | bytes accessed | tf_op | source)
XLA Modules:
  0.0 109.7 jit_solution(16809010216716755276)
XLA Ops:
  0.6 0.8 dynamic-slice_compare_fusion
  1.4 0.1 broadcast_in_dim.14
  1.5 0.1 reshape.54
  1.6 0.1 copy.43
  1.7 0.6 pad_select_fusion.bias_ref
  2.3 1.1 broadcast_multiply_fusion
  3.4 0.1 reshape.52
  3.5 0.1 copy.39
  3.7 0.0 copy-start
  3.7 0.9 copy-done
  4.6 0.1 reshape.50
  4.7 0.1 copy.35
  4.8 0.0 copy-start.1
  4.9 0.9 copy-done.1
  5.8 0.1 reshape.51
  5.9 0.1 copy.36
  6.0 0.0 copy-start.2
  6.1 0.9 copy-done.2
  7.0 0.1 reshape.53
  7.1 0.1 copy.40
  7.3 1.1 %pad_maximum_fusion = (bf16[4,2,3,48,256]{4,3,2,1,0:T(8,128)(2,1)}, bf16[4,2,3,48,256]{4,3,2,1,0:T(8,128)(2,1)}) fusion(bf16[4,1,3,48,256]{4,3,2,1,0:T(8,128)(2,1)S(1)} %copy.38, bf16[4,1,3,48,256]{4,3,2,1,0:T(8,128)(2,1)S(1)} %copy.37, bf16[4,1,3,48,256]{4,3,2,1,0:T(8,128)(2,1)S(1)} %copy.42, bf16[4,1,3,48,256]{4,3,2,1,0:T(8,128)(2,1)S(1)} %copy.41), kind=kLoop, calls=%fused_computation | loop fusion | flops 589824 | bytes 2359296 | tf_op jit(solution)/shard_map/stack | solution.py:328
  8.4 95.5 %butterfly.1 = (bf16[4,3,48,256]{3,2,1,0:T(8,128)(2,1)}, bf16[4,3,48,256]{3,2,1,0:T(8,128)(2,1)}, bf16[4,3,48,256]{3,2,1,0:T(8,128)(2,1)}, bf16[4,3,48,256]{3,2,1,0:T(8,128)(2,1)}) custom-call(bf16[4,2,3,48,256]{4,3,2,1,0:T(8,128)(2,1)} %get-tuple-element.16.kv_ref, bf16[4,2,3,48,256]{4,3,2,1,0:T(8,128)(2,1)} %get-tuple-element.17.qg_ref, ...), custom_call_target="tpu_custom_call" | custom-call | tf_op jit(solution)/shard_map/butterfly/pallas_call | solution.py:341
  103.9 1.1 %copy.44 = bf16[4,3,48,256]{3,0,2,1:T(4,128)(2,1)S(1)} copy(bf16[4,3,48,256]{3,2,1,0:T(8,128)(2,1)} %get-tuple-element.8) | data formatting | bytes 589824 | tf_op jit(solution)/shard_map/butterfly/pallas_call | solution.py:341
  105.0 0.1 copy.45
  105.1 0.0 copy-start.5
  105.1 0.8 reshape.57
  106.0 0.1 copy-done.5
  106.1 0.2 copy.46
  106.3 0.1 copy.47
  106.4 0.0 copy-start.4
  106.4 0.8 reshape.59
  107.2 0.1 copy-done.4
  107.3 0.2 copy.48
  107.5 0.1 copy.49
  107.6 0.0 copy-start.3
  107.6 0.8 reshape.61
  108.4 0.1 copy-done.3
  108.6 0.2 copy.50
  108.7 0.1 copy.51
  108.8 0.8 reshape.63
  (6 shorter events, 0.2 us)
Async XLA Ops:
  3.7 1.0 copy-start
  4.8 1.0 copy-start.1
  6.0 1.0 copy-start.2
  105.1 1.0 copy-start.5
  106.4 1.0 copy-start.4
  107.6 1.0 copy-start.3
where the time goes:
time: 110 us
  Pallas kernels  95.5 us (87%)
  local copies, waits for them, and re-layouts  9.72 us (9%)
  other arithmetic  3.61 us (3%)
    pallas_call x1, Pallas kernels, per_device(): pl.pallas_call(functools.partial(kernel, dims), out_shape=(out,) * 4, in_...  95.5 us
    reshape x4, local copies, waits for them, and re-layouts, back(): array.reshape(chunks, rows, frames, cols, WIDE).transpose(2, 1, 3, 0, 4)  3.31 us
    unnamed x12, local copies, waits for them, and re-layouts  3.13 us

commit v1 on v0

--- a/solution.py
+++ b/solution.py
@@ -10,9 +10,10 @@
 HEAD_DIM = 64
 SCALE = 0.125
 NEG = -1e30
+AHEAD = 2
 WIDE = 256
 HEADS = WIDE // HEAD_DIM
-STATS = 3 * HEADS
+STATS = 4 * HEADS
 F32 = jnp.float32
 BF16 = jnp.bfloat16
 
@@ -30,12 +31,13 @@
 
 
 def kernel(
-    dims, kv_ref, qg_ref, bias_ref, o_ref, dq_ref, dk_ref, dv_ref,
-    kvx, halo, qm, gm, pm, ot, stat, stat_in, wm, dm, oq, rim_out, rim_in, dkv, dkv_out, dkv_in,
-    kv_ss, kv_rs, halo_ss, halo_rs, stat_ss, stat_rs, rim_ss, rim_rs, dkv_ss, dkv_rs,
+    dims, q_hbm, k_hbm, v_hbm, g_hbm, mask_hbm, out_ref,
+    k_ref, v_ref, q_ref, g_ref, mask_ref, kvx, qg, halo, bias_at, qm, gm, pm, ot, stat, stat_in, wm, dm, oq, rim_out, rim_in, dkv, dkv_out, dkv_in,
+    kv_ss, kv_rs, halo_ss, halo_rs, stat_ss, stat_rs, rim_ss, rim_rs, dkv_ss, dkv_rs, load_sem,
 ):
     chunks, rows, tok, bits, space, keys = dims
     ext = rows + 2
+    frames = q_ref.shape[2]
     frame_at = lax.axis_index("frame")
     space_at = lax.axis_index("space")
     partner = []
@@ -53,7 +55,7 @@
 
     def kv_copy(c, b):
         return remote(
-            kv_ref.at[c], kvx.at[c, :, :, pl.ds(tok * (b + 1), tok)],
+            kvx.at[c, :, :, pl.ds(0, tok)], kvx.at[c, :, :, pl.ds(tok * (b + 1), tok)],
             kv_ss.at[c, b], kv_rs.at[c, b], partner[b], space_at,
         )
 
@@ -64,7 +66,7 @@
 
     def halo_copy(c, s):
         return remote(
-            qg_ref.at[c, :, 0 if s == 0 else rows - 1], halo.at[c, 1 - s],
+            qg.at[c, :, 0 if s == 0 else rows - 1], halo.at[c, 1 - s],
             halo_ss.at[c, s], halo_rs.at[c, 1 - s], frame_at, near[s],
         )
 
@@ -97,6 +99,15 @@
             @pl.when(has[s])
             def _():
                 copy(c, s).wait_send()
+
+    loads = [
+        pltpu.make_async_copy(source, target, load_sem.at[n])
+        for n, (source, target) in enumerate(
+            ((k_hbm, k_ref), (v_hbm, v_ref), (q_hbm, q_ref), (g_hbm, g_ref), (mask_hbm, mask_ref))
+        )
+    ]
+    for load in loads:
+        load.start()
 
     barrier = pltpu.get_barrier_semaphore()
     for b in range(bits):
@@ -109,28 +120,51 @@
             pl.semaphore_signal(
                 barrier, inc=1, device_id=(frame_at, near[s]), device_id_type=pl.DeviceIdType.MESH
             )
+    for load in loads:
+        load.wait()
+
+    def gather(c, carry):
+        at = pl.ds(pl.multiple_of(c * WIDE, WIDE), WIDE)
+        for r in range(rows):
+            kvx[c, 0, r, :tok] = k_ref[r, :, :, at].reshape(tok, WIDE)
+            kvx[c, 1, r, :tok] = v_ref[r, :, :, at].reshape(tok, WIDE)
+            query = q_ref[r, :, :, at].reshape(tok, WIDE)
+            qg[c, 0, r] = (query.astype(F32) * SCALE).astype(BF16)
+            qg[c, 1, r] = g_ref[r, :, :, at].reshape(tok, WIDE)
+        return carry
+
+    lax.fori_loop(0, chunks, gather, 0)
+
     pl.semaphore_wait(barrier, bits + has[0].astype(jnp.int32) + has[1].astype(jnp.int32))
 
     def send_first(c, carry):
+        start_sides(halo_copy, c)
         for b in reversed(range(bits)):
             kv_copy(c, b).start()
-        start_sides(halo_copy, c)
-        return carry
-
-    lax.fori_loop(0, chunks, send_first, 0)
-
-    lane = lax.broadcasted_iota(jnp.int32, (tok, 128), 1)
-    low = lane < HEAD_DIM
+        return carry
+
+    lax.fori_loop(0, min(AHEAD, chunks), send_first, 0)
+
+    low = lax.broadcasted_iota(jnp.int32, (tok, 128), 1) < HEAD_DIM
 
     for s in range(2):
         @pl.when(jnp.logical_not(has[s]))
         def _():
             halo[:, s] = jnp.zeros(halo.shape[:1] + halo.shape[2:], BF16)
             rim_in[:, s] = jnp.zeros(rim_in.shape[:1] + rim_in.shape[2:], BF16)
-            top_lane = lane - (lane // STATS) * STATS < HEADS
-            stat_in[:, s] = jnp.broadcast_to(
-                jnp.where(top_lane, NEG, 0.0).astype(F32)[None], (chunks, tok, 128)
-            )
+            stat_row = lax.broadcasted_iota(jnp.int32, (chunks, STATS, 128), 1)
+            stat_in[:, s] = jnp.where(stat_row < HEADS, NEG, 0.0).astype(F32)
+
+    every = mask_ref.shape[1]
+    token = lax.broadcasted_iota(jnp.int32, (tok, every), 0)
+    here = lax.broadcasted_iota(jnp.int32, (tok, every), 1) == frame_at * frames + token % frames
+    slot = lax.broadcasted_iota(jnp.int32, (tok, keys), 1) // tok
+    bias = jnp.where(slot > bits, NEG, 0.0).astype(F32)
+    for b in range(bits):
+        chosen = jnp.where(here, mask_ref[b : b + 1, :].astype(F32), 0.0)
+        open_to = jnp.sum(chosen, axis=1, keepdims=True)
+        bias = jnp.where(slot == b + 1, (1.0 - open_to) * NEG, bias)
+    bias_at[...] = bias
 
     def stacked(block):
         wide = block.astype(F32)
@@ -151,22 +185,29 @@
             axis=1,
         )
 
-    def forward(c):
-        kvx[c, :, :, :tok, :] = kv_ref[c]
+    def prepare(c, carry):
         spare = keys - tok * (bits + 1)
         if spare:
             kvx[c, :, :, keys - spare :, :] = jnp.zeros((2, rows, spare, WIDE), BF16)
-        bias = jnp.concatenate([bias_ref[...]] * HEADS, axis=0)
-        tiles = [jnp.zeros((tok, 128), F32) for _ in range(3)]
+        for r in range(rows):
+            qm[c, r + 1] = stacked(qg[c, 0, r])
+            gm[c, r + 1] = stacked(qg[c, 1, r])
+        return carry
+
+    lax.fori_loop(0, chunks, prepare, 0)
+
+    stat_lane = lax.broadcasted_iota(jnp.int32, (tok, 128), 1)
+    spare_tokens = jnp.zeros((128 - 2 * tok, 128), F32)
+
+    def forward(c):
+        bias = jnp.concatenate([bias_at[...]] * HEADS, axis=0)
+        tiles = []
         for i in range(ext):
             if i == 0 or i == ext - 1:
-                query, grad = halo[c, 0 if i == 0 else 1, 0], halo[c, 0 if i == 0 else 1, 1]
-            else:
-                query, grad = qg_ref[c, 0, i - 1], qg_ref[c, 1, i - 1]
-            query = stacked(query)
-            grad = stacked(grad)
-            qm[c, i] = query
-            gm[c, i] = grad
+                side = 0 if i == 0 else 1
+                qm[c, i] = stacked(halo[c, side, 0])
+                gm[c, i] = stacked(halo[c, side, 1])
+            query, grad = qm[c, i], gm[c, i]
             near_rows = [r for r in range(rows) if 0 <= i - r <= 2]
             scores = [dot_nt(query, kvx[c, 0, r]) + bias for r in near_rows]
             top = jnp.max(functools.reduce(jnp.maximum, scores), axis=1, keepdims=True)
@@ -179,8 +220,7 @@
                 part = dot_nn(prob, kvx[c, 1, r])
                 full = part if full is None else full + part
             ot[c, i] = picked(full)
-            place = 0 if i < 2 else (1 if i < ext - 2 else 2)
-            base = STATS * (1 if i in (1, ext - 1) else 0)
+            tile = jnp.zeros((tok, 128), F32)
             for h in range(HEADS):
                 span = slice(h * tok, (h + 1) * tok)
                 half = slice(128 * (h // 2), 128 * (h // 2) + 128)
@@ -188,36 +228,40 @@
                     full[span, half] * grad[span, half].astype(F32), axis=1, keepdims=True
                 )
                 for kind, value in enumerate((top[span], total[span], delta)):
-                    tiles[place] = jnp.where(lane == base + kind * HEADS + h, value, tiles[place])
-        for place in range(3):
-            stat[c, place] = tiles[place]
+                    tile = jnp.where(stat_lane == kind * HEADS + h, value, tile)
+            tiles.append(tile)
+        for place, at in enumerate((0, 2, ext - 2)):
+            second = tiles[at + 1] if place != 1 else jnp.zeros((tok, 128), F32)
+            both = jnp.concatenate([tiles[at], second, spare_tokens], axis=0)
+            stat[c, place] = both.T[:STATS]
 
     def backward(c):
-        alphas, deltas = [], []
+        turned = []
         for place in range(3):
             mine = stat[c, place]
-            top, total, delta = mine, pltpu.roll(mine, 128 - HEADS, 1), pltpu.roll(mine, 128 - 2 * HEADS, 1)
+            top, total, delta = (mine[k * HEADS : (k + 1) * HEADS] for k in range(3))
             if place == 1:
-                alphas.append(1.0 / total)
-                deltas.append(delta / total)
-                continue
-            theirs = stat_in[c, 0 if place == 0 else 1]
-            top2, total2, delta2 = (
-                theirs, pltpu.roll(theirs, 128 - HEADS, 1), pltpu.roll(theirs, 128 - 2 * HEADS, 1)
+                alpha = 1.0 / total
+                delta = delta * alpha
+            else:
+                theirs = stat_in[c, place // 2]
+                top2, total2, delta2 = (theirs[k * HEADS : (k + 1) * HEADS] for k in range(3))
+                best = jnp.maximum(top, top2)
+                part, part2 = jnp.exp(top - best), jnp.exp(top2 - best)
+                inverse = 1.0 / (total * part + total2 * part2)
+                alpha = part * inverse
+                delta = (delta * part + delta2 * part2) * inverse
+            both = jnp.concatenate(
+                [alpha, delta, jnp.zeros((128 - 2 * HEADS, 128), F32)], axis=0
             )
-            best = jnp.maximum(top, top2)
-            part, part2 = jnp.exp(top - best), jnp.exp(top2 - best)
-            inverse = 1.0 / (total * part + total2 * part2)
-            alphas.append(part * inverse)
-            deltas.append((delta * part + delta2 * part2) * inverse)
+            turned.append(both.T)
         for i in range(ext):
             place = 0 if i < 2 else (1 if i < ext - 2 else 2)
-            base = STATS * (1 if i in (1, ext - 1) else 0)
-            alpha_h = [alphas[place][:, base + h : base + h + 1] for h in range(HEADS)]
+            base = tok if i in (1, ext - 1) else 0
+            columns = turned[place][base : base + tok]
+            alpha_h = [columns[:, h : h + 1] for h in range(HEADS)]
             alpha = jnp.concatenate(alpha_h, axis=0)
-            delta = jnp.concatenate(
-                [deltas[place][:, base + h : base + h + 1] for h in range(HEADS)], axis=0
-            )
+            delta = jnp.concatenate([columns[:, HEADS + h : HEADS + h + 1] for h in range(HEADS)], axis=0)
             full = None
             for r in range(rows):
                 if not 0 <= i - r <= 2:
@@ -256,6 +300,11 @@
         def _():
             for b in range(bits):
                 kv_copy(t, b).wait_recv()
+
+            @pl.when(t + AHEAD < chunks)
+            def _():
+                send_first(t + AHEAD, 0)
+
             wait_sides(halo_copy, t)
             forward(t)
             start_sides(stat_copy, t)
@@ -273,23 +322,25 @@
     lax.fori_loop(0, chunks + 1, step, 0)
 
     def finish(c, carry):
+        at = pl.ds(pl.multiple_of(c * WIDE, WIDE), WIDE)
+        shape = (tok // frames, frames, WIDE)
         wait_sides(rim_copy, c)
         for r in range(rows):
-            for which, out in enumerate((o_ref, dq_ref)):
+            for which in range(2):
                 result = oq[c, which, r]
                 if r == 0:
                     result = result + rim_in[c, 0, which].astype(F32)
                 if r == rows - 1:
                     result = result + rim_in[c, 1, which].astype(F32)
-                out[c, r] = result.astype(BF16)
+                out_ref[which, r, :, :, at] = result.astype(BF16).reshape(shape)
         for b in range(bits):
             dkv_copy(c, b).wait_recv()
         for r in range(rows):
-            for which, out in enumerate((dk_ref, dv_ref)):
+            for which in range(2):
                 result = dkv[c, which, r]
                 for b in range(bits):
                     result = result + dkv_in[c, b, which, r].astype(F32)
-                out[c, r] = result.astype(BF16)
+                out_ref[2 + which, r, :, :, at] = result.astype(BF16).reshape(shape)
         return carry
 
     lax.fori_loop(0, chunks, finish, 0)
@@ -304,6 +355,21 @@
         return carry
 
     lax.fori_loop(0, chunks, drain, 0)
+
+
+def settle(in_ref, *refs):
+    outs, (held, in_sem, out_sem) = refs[:-3], refs[-3:]
+    fetches = [
+        pltpu.make_async_copy(in_ref.at[n], held.at[n], in_sem.at[n]) for n in range(len(outs))
+    ]
+    stores = [pltpu.make_async_copy(held.at[n], out, out_sem.at[n]) for n, out in enumerate(outs)]
+    for fetch in fetches:
+        fetch.start()
+    for fetch, store in zip(fetches, stores):
+        fetch.wait()
+        store.start()
+    for store in stores:
+        store.wait()
 
 
 def per_device(query_vectors, key_vectors, value_vectors, out_cotangent, partner_mask):
@@ -314,44 +380,33 @@
     tok = frames * cols
     keys = -(-tok * (bits + 1) // 128) * 128
     ext = rows + 2
-
-    def lay(array):
-        return array.reshape(frames, rows, cols, chunks, WIDE).transpose(3, 1, 0, 2, 4).reshape(
-            chunks, rows, tok, WIDE
-        )
-
-    def back(array):
-        return array.reshape(chunks, rows, frames, cols, WIDE).transpose(2, 1, 3, 0, 4).reshape(
-            frames, rows, cols, width
-        )
-
-    kv = jnp.stack([lay(key_vectors), lay(value_vectors)], axis=1)
-    qg = jnp.stack([lay(query_vectors * SCALE), lay(out_cotangent)], axis=1)
-    own = lax.dynamic_slice_in_dim(partner_mask, lax.axis_index("frame") * frames, frames, 0)[:, :bits] == 1
-    allowed = jnp.concatenate([jnp.ones((frames, 1), bool), own], axis=1)
-    allowed = jnp.repeat(jnp.repeat(allowed, cols, axis=0), tok, axis=1)
-    allowed = jnp.pad(allowed, ((0, 0), (0, keys - allowed.shape[1])))
-    bias = jnp.where(allowed, 0.0, NEG).astype(F32)
+    arrays = [
+        array.transpose(1, 2, 0, 3)
+        for array in (query_vectors, key_vectors, value_vectors, out_cotangent)
+    ]
 
     dims = (chunks, rows, tok, bits, space, keys)
-    out = jax.ShapeDtypeStruct((chunks, rows, tok, WIDE), BF16)
     vmem = pl.BlockSpec(memory_space=pltpu.VMEM)
     stack = HEADS * tok
     dma = pltpu.SemaphoreType.DMA
-    results = pl.pallas_call(
+    result = pl.pallas_call(
         functools.partial(kernel, dims),
-        out_shape=(out,) * 4,
-        in_specs=[vmem] * 3,
-        out_specs=(vmem,) * 4,
+        out_shape=jax.ShapeDtypeStruct((4, rows, cols, frames, width), BF16),
+        in_specs=[pl.BlockSpec(memory_space=pl.ANY)] * 5,
+        out_specs=vmem,
         scratch_shapes=[
+            *[pltpu.VMEM((rows, cols, frames, width), BF16)] * 4,
+            pltpu.VMEM(partner_mask.shape[::-1], jnp.int32),
             pltpu.VMEM((chunks, 2, rows, keys, WIDE), BF16),
+            pltpu.VMEM((chunks, 2, rows, tok, WIDE), BF16),
             pltpu.VMEM((chunks, 2, 2, tok, WIDE), BF16),
+            pltpu.VMEM((tok, keys), F32),
             pltpu.VMEM((chunks, ext, stack, WIDE), BF16),
             pltpu.VMEM((chunks, ext, stack, WIDE), BF16),
             pltpu.VMEM((chunks, rows, 3, stack, keys), BF16),
             pltpu.VMEM((chunks, ext, tok, WIDE), F32),
-            pltpu.VMEM((chunks, 3, tok, 128), F32),
-            pltpu.VMEM((chunks, 2, tok, 128), F32),
+            pltpu.VMEM((chunks, 3, STATS, 128), F32),
+            pltpu.VMEM((chunks, 2, STATS, 128), F32),
             pltpu.VMEM((rows, 3, stack, keys), BF16),
             pltpu.VMEM((rows, 3, stack, keys), BF16),
             pltpu.VMEM((chunks, 2, rows, tok, WIDE), F32),
@@ -365,13 +420,23 @@
             dma((chunks, 2)), dma((chunks, 2)),
             dma((chunks, 2)), dma((chunks, 2)),
             dma((chunks, bits)), dma((chunks, bits)),
+            dma((5,)),
         ],
         compiler_params=pltpu.CompilerParams(
-            collective_id=0, has_side_effects=True, vmem_limit_bytes=56 * 1024 * 1024
+            collective_id=0, has_side_effects=True, vmem_limit_bytes=60 * 1024 * 1024
         ),
         name="butterfly",
-    )(kv, qg, bias)
-    return tuple(back(result) for result in results)
+    )(*arrays, partner_mask.T)
+    where = pl.BlockSpec(memory_space=pl.ANY)
+    outs = pl.pallas_call(
+        settle,
+        out_shape=(jax.ShapeDtypeStruct((rows, cols, frames, width), BF16),) * 4,
+        in_specs=[where],
+        out_specs=(where,) * 4,
+        scratch_shapes=[pltpu.VMEM((4, rows, cols, frames, width), BF16), dma((4,)), dma((4,))],
+        name="settle",
+    )(result)
+    return tuple(out.transpose(2, 0, 1, 3) for out in outs)
 
 
 def solution(mesh):

time: 110 us -> 91.3 us (0.83)
  the two profiles are of different devices: /device:TPU:67 before, /device:TPU:1 now
where the time goes in v1:
time: 91.3 us; the launch traced here: 91.2 us
  Pallas kernels  90.5 us (99%)
    pallas_call x1, Pallas kernels, per_device(): pl.pallas_call(functools.partial(kernel, dims), out_shape=jax.ShapeDtypeS...  88.5 us
    pallas_call x1, Pallas kernels, per_device(): pl.pallas_call(settle, out_shape=(jax.ShapeDtypeStruct((rows, cols, frame...  2.04 us

profile of v1, /device:TPU:1, one launch (start us, length us, event | category | flops | bytes accessed | tf_op | source)
XLA Modules:
  0.0 91.2 jit_solution(7234673447632267659)
XLA Ops:
  0.6 88.5 %butterfly.1.in_ref = bf16[4,3,12,4,1024]{4,3,2,1,0:T(4,128)(2,1)} custom-call(bf16[3,12,4,1024]{3,2,1,0:T(4,128)(2,1)} %bitcast.9, bf16[3,12,4,1024]{3,2,1,0:T(4,128)(2,1)} %bitcast.10, bf16[3,12,4,1024]{3,2,1,0:T(4,128)(2,1)} %bitcast.11, bf16[3,12,4,1024]{3,2,1,0:T(4,128)(2,1)} %bitcast.12, s32[4,512]{1,0:T(4,128)} %bitcast.13), custom_call_target="tpu_custom_call" | custom-call | tf_op jit(solution)/shard_map/butterfly/pallas_call | solution.py:392
  89.1 2.0 %settle.1 = (bf16[3,12,4,1024]{3,2,1,0:T(4,128)(2,1)}, bf16[3,12,4,1024]{3,2,1,0:T(4,128)(2,1)}, bf16[3,12,4,1024]{3,2,1,0:T(4,128)(2,1)}, bf16[3,12,4,1024]{3,2,1,0:T(4,128)(2,1)}) custom-call(bf16[4,3,12,4,1024]{4,3,2,1,0:T(4,128)(2,1)} %butterfly.1.in_ref), custom_call_target="tpu_custom_call" | custom-call | tf_op jit(solution)/shard_map/settle/pallas_call | solution.py:431

commit v2 on v1

--- a/solution.py
+++ b/solution.py
@@ -14,6 +14,7 @@
 WIDE = 256
 HEADS = WIDE // HEAD_DIM
 STATS = 4 * HEADS
+SENT = 2 * HEADS
 F32 = jnp.float32
 BF16 = jnp.bfloat16
 
@@ -72,7 +73,7 @@
 
     def stat_copy(c, s):
         return remote(
-            stat.at[c, 2 * s], stat_in.at[c, 1 - s],
+            stat.at[c, 2 * s, pl.ds(0, SENT)], stat_in.at[c, 1 - s],
             stat_ss.at[c, s], stat_rs.at[c, 1 - s], frame_at, near[s],
         )
 
@@ -133,7 +134,7 @@
             qg[c, 1, r] = g_ref[r, :, :, at].reshape(tok, WIDE)
         return carry
 
-    lax.fori_loop(0, chunks, gather, 0)
+    gather(0, 0)
 
     pl.semaphore_wait(barrier, bits + has[0].astype(jnp.int32) + has[1].astype(jnp.int32))
 
@@ -143,7 +144,18 @@
             kv_copy(c, b).start()
         return carry
 
-    lax.fori_loop(0, min(AHEAD, chunks), send_first, 0)
+    send_first(0, 0)
+
+    def gather_on(c, carry):
+        gather(c, 0)
+
+        @pl.when(c < AHEAD)
+        def _():
+            send_first(c, 0)
+
+        return carry
+
+    lax.fori_loop(1, chunks, gather_on, 0)
 
     low = lax.broadcasted_iota(jnp.int32, (tok, 128), 1) < HEAD_DIM
 
@@ -152,7 +164,7 @@
         def _():
             halo[:, s] = jnp.zeros(halo.shape[:1] + halo.shape[2:], BF16)
             rim_in[:, s] = jnp.zeros(rim_in.shape[:1] + rim_in.shape[2:], BF16)
-            stat_row = lax.broadcasted_iota(jnp.int32, (chunks, STATS, 128), 1)
+            stat_row = lax.broadcasted_iota(jnp.int32, (chunks, SENT, 128), 1)
             stat_in[:, s] = jnp.where(stat_row < HEADS, NEG, 0.0).astype(F32)
 
     every = mask_ref.shape[1]
@@ -220,14 +232,16 @@
                 part = dot_nn(prob, kvx[c, 1, r])
                 full = part if full is None else full + part
             ot[c, i] = picked(full)
+            inverse = 1.0 / total
+            log_total = top + jnp.log(total)
             tile = jnp.zeros((tok, 128), F32)
             for h in range(HEADS):
                 span = slice(h * tok, (h + 1) * tok)
                 half = slice(128 * (h // 2), 128 * (h // 2) + 128)
-                delta = jnp.sum(
+                delta = inverse[span] * jnp.sum(
                     full[span, half] * grad[span, half].astype(F32), axis=1, keepdims=True
                 )
-                for kind, value in enumerate((top[span], total[span], delta)):
+                for kind, value in enumerate((log_total[span], delta, top[span])):
                     tile = jnp.where(stat_lane == kind * HEADS + h, value, tile)
             tiles.append(tile)
         for place, at in enumerate((0, 2, ext - 2)):
@@ -239,18 +253,15 @@
         turned = []
         for place in range(3):
             mine = stat[c, place]
-            top, total, delta = (mine[k * HEADS : (k + 1) * HEADS] for k in range(3))
-            if place == 1:
-                alpha = 1.0 / total
-                delta = delta * alpha
-            else:
+            log_total, delta, top = (mine[k * HEADS : (k + 1) * HEADS] for k in range(3))
+            if place != 1:
                 theirs = stat_in[c, place // 2]
-                top2, total2, delta2 = (theirs[k * HEADS : (k + 1) * HEADS] for k in range(3))
-                best = jnp.maximum(top, top2)
-                part, part2 = jnp.exp(top - best), jnp.exp(top2 - best)
-                inverse = 1.0 / (total * part + total2 * part2)
-                alpha = part * inverse
-                delta = (delta * part + delta2 * part2) * inverse
+                log_total2, delta2 = (theirs[k * HEADS : (k + 1) * HEADS] for k in range(2))
+                best = jnp.maximum(log_total, log_total2)
+                part, part2 = jnp.exp(log_total - best), jnp.exp(log_total2 - best)
+                delta = (delta * part + delta2 * part2) / (part + part2)
+                log_total = best + jnp.log(part + part2)
+            alpha = jnp.exp(top - log_total)
             both = jnp.concatenate(
                 [alpha, delta, jnp.zeros((128 - 2 * HEADS, 128), F32)], axis=0
             )
@@ -285,6 +296,7 @@
             else:
                 oq[c, 0, i - 1] = attended
                 oq[c, 1, i - 1] = query_grad
+        start_sides(rim_copy, c)
         for r in range(rows):
             grads = gm[c, r : r + 3].reshape(3 * HEADS * tok, WIDE)
             queries = qm[c, r : r + 3].reshape(3 * HEADS * tok, WIDE)
@@ -315,7 +327,6 @@
             backward(t - 1)
             for b in reversed(range(bits)):
                 dkv_copy(t - 1, b).start()
-            start_sides(rim_copy, t - 1)
 
         return carry
 
@@ -406,7 +417,7 @@
             pltpu.VMEM((chunks, rows, 3, stack, keys), BF16),
             pltpu.VMEM((chunks, ext, tok, WIDE), F32),
             pltpu.VMEM((chunks, 3, STATS, 128), F32),
-            pltpu.VMEM((chunks, 2, STATS, 128), F32),
+            pltpu.VMEM((chunks, 2, SENT, 128), F32),
             pltpu.VMEM((rows, 3, stack, keys), BF16),
             pltpu.VMEM((rows, 3, stack, keys), BF16),
             pltpu.VMEM((chunks, 2, rows, tok, WIDE), F32),

time: 91.3 us -> 88.9 us (0.974)
  Pallas kernels: 90.5 us -> 88.1 us
    pallas_call x1, Pallas kernels: 88.5 us -> 86.1 us  [per_device(): pl.pallas_call(functools.partial(kernel, dims), out_shape=jax.ShapeDtypeS...]
where the time goes in v2:
time: 88.9 us; the launch traced here: 88.8 us
  Pallas kernels  88.1 us (99%)
    pallas_call x1, Pallas kernels, per_device(): pl.pallas_call(functools.partial(kernel, dims), out_shape=jax.ShapeDtypeS...  86.1 us
    pallas_call x1, Pallas kernels, per_device(): pl.pallas_call(settle, out_shape=(jax.ShapeDtypeStruct((rows, cols, frame...  2.04 us

profile of v2, /device:TPU:1, one launch (start us, length us, event | category | flops | bytes accessed | tf_op | source)
XLA Modules:
  0.0 88.8 jit_solution(16437155207808515854)
XLA Ops:
  0.6 86.1 %butterfly.1.in_ref = bf16[4,3,12,4,1024]{4,3,2,1,0:T(4,128)(2,1)} custom-call(bf16[3,12,4,1024]{3,2,1,0:T(4,128)(2,1)} %bitcast.9, bf16[3,12,4,1024]{3,2,1,0:T(4,128)(2,1)} %bitcast.10, bf16[3,12,4,1024]{3,2,1,0:T(4,128)(2,1)} %bitcast.11, bf16[3,12,4,1024]{3,2,1,0:T(4,128)(2,1)} %bitcast.12, s32[4,512]{1,0:T(4,128)} %bitcast.13), custom_call_target="tpu_custom_call" | custom-call | tf_op jit(solution)/shard_map/butterfly/pallas_call | solution.py:403
  86.7 2.0 %settle.1 = (bf16[3,12,4,1024]{3,2,1,0:T(4,128)(2,1)}, bf16[3,12,4,1024]{3,2,1,0:T(4,128)(2,1)}, bf16[3,12,4,1024]{3,2,1,0:T(4,128)(2,1)}, bf16[3,12,4,1024]{3,2,1,0:T(4,128)(2,1)}) custom-call(bf16[4,3,12,4,1024]{4,3,2,1,0:T(4,128)(2,1)} %butterfly.1.in_ref), custom_call_target="tpu_custom_call" | custom-call | tf_op jit(solution)/shard_map/settle/pallas_call | solution.py:442

commit v3 on v2

--- a/solution.py
+++ b/solution.py
@@ -227,9 +227,8 @@
             total = jnp.sum(functools.reduce(jnp.add, probs), axis=1, keepdims=True)
             full = None
             for r, prob in zip(near_rows, probs):
-                prob = prob.astype(BF16)
                 pm[c, r, i - r] = prob
-                part = dot_nn(prob, kvx[c, 1, r])
+                part = dot_nn(prob.astype(BF16), kvx[c, 1, r])
                 full = part if full is None else full + part
             ot[c, i] = picked(full)
             inverse = 1.0 / total
@@ -278,7 +277,7 @@
                 if not 0 <= i - r <= 2:
                     continue
                 grad_prob = dot_nt(gm[c, i], kvx[c, 1, r])
-                weight = pm[c, r, i - r].astype(F32) * alpha
+                weight = pm[c, r, i - r] * alpha
                 grad_score = (weight * (grad_prob - delta)).astype(BF16)
                 wm[r, i - r] = weight.astype(BF16)
                 dm[r, i - r] = grad_score
@@ -414,7 +413,7 @@
             pltpu.VMEM((tok, keys), F32),
             pltpu.VMEM((chunks, ext, stack, WIDE), BF16),
             pltpu.VMEM((chunks, ext, stack, WIDE), BF16),
-            pltpu.VMEM((chunks, rows, 3, stack, keys), BF16),
+            pltpu.VMEM((chunks, rows, 3, stack, keys), F32),
             pltpu.VMEM((chunks, ext, tok, WIDE), F32),
             pltpu.VMEM((chunks, 3, STATS, 128), F32),
             pltpu.VMEM((chunks, 2, SENT, 128), F32),

time: 88.9 us -> 88.9 us (level)
  no operation moved by 1% of the time
where the time goes in v3:
time: 88.9 us; the launch traced here: 88.7 us
  Pallas kernels  88.1 us (99%)
    pallas_call x1, Pallas kernels, per_device(): pl.pallas_call(functools.partial(kernel, dims), out_shape=jax.ShapeDtypeS...  86 us
    pallas_call x1, Pallas kernels, per_device(): pl.pallas_call(settle, out_shape=(jax.ShapeDtypeStruct((rows, cols, frame...  2.04 us

profile of v3, /device:TPU:1, one launch (start us, length us, event | category | flops | bytes accessed | tf_op | source)
XLA Modules:
  0.0 88.7 jit_solution(2449920326285687016)
XLA Ops:
  0.6 86.0 %butterfly.1.in_ref = bf16[4,3,12,4,1024]{4,3,2,1,0:T(4,128)(2,1)} custom-call(bf16[3,12,4,1024]{3,2,1,0:T(4,128)(2,1)} %bitcast.9, bf16[3,12,4,1024]{3,2,1,0:T(4,128)(2,1)} %bitcast.10, bf16[3,12,4,1024]{3,2,1,0:T(4,128)(2,1)} %bitcast.11, bf16[3,12,4,1024]{3,2,1,0:T(4,128)(2,1)} %bitcast.12, s32[4,512]{1,0:T(4,128)} %bitcast.13), custom_call_target="tpu_custom_call" | custom-call | tf_op jit(solution)/shard_map/butterfly/pallas_call | solution.py:402
  86.7 2.0 %settle.1 = (bf16[3,12,4,1024]{3,2,1,0:T(4,128)(2,1)}, bf16[3,12,4,1024]{3,2,1,0:T(4,128)(2,1)}, bf16[3,12,4,1024]{3,2,1,0:T(4,128)(2,1)}, bf16[3,12,4,1024]{3,2,1,0:T(4,128)(2,1)}) custom-call(bf16[4,3,12,4,1024]{4,3,2,1,0:T(4,128)(2,1)} %butterfly.1.in_ref), custom_call_target="tpu_custom_call" | custom-call | tf_op jit(solution)/shard_map/settle/pallas_call | solution.py:441
